TPU v7x, 32 devices: a whole 2x2x4 slice. The times are simulated.
32 devices in a mesh: groups: 2 (over x), gx: 16 (over z, y, core).
Axes of the slice: x: 2, y: 2, z: 4, core: 2. Of those that a mesh axis runs over, the one named last changes fastest.
Arguments:
- east_current: float32 [512, 32], P(('groups', 'gx')), parts along dimension 0, may hold values from -0.2 to 0.2
- north_current: float32 [512, 32], P(('groups', 'gx')), parts along dimension 0, may hold values from -0.2 to 0.2
- land_mask: int32 [512, 32], P(('groups', 'gx')), parts along dimension 0, may hold values 0 or 1
- spectrum: bfloat16 [1296, 64, 256], P(None, ('groups', 'gx')), parts along dimension 1, may hold values from 0.049804688 to 1
- spectral_in: bfloat16 [256, 1296], replicated, may hold values from -0.15625 to 0.15625
- spectral_out: bfloat16 [1296, 256], replicated, may hold values from -0.375 to 0.375
- conv_first: bfloat16 [64, 18], replicated, may hold values from -1.5 to 1.5
- conv_second: bfloat16 [64, 576], replicated, may hold values from -0.25 to 0.25
- conv_last: bfloat16 [2, 64], replicated, may hold values from -0.75 to 0.75
Outputs:
- east_next: float32 [512, 32], P(('groups', 'gx')), parts along dimension 0
- north_next: float32 [512, 32], P(('groups', 'gx')), parts along dimension 0
- new_spectrum: bfloat16 [1296, 64, 256], P(None, ('groups', 'gx')), parts along dimension 1
There are 2 independent parts, one for each index of `groups`. A program takes and returns all parts, laid end to end along the dimension named above; an argument that names none is the same for every part. Nothing has to cross between parts.
All inputs are finite; a program needn't handle non-finite values. No bound on the sum of `land_mask` on one device may be relied on, other than what follows from the above.
Results may differ from a plain program's by a relative error of at most 0.0052.
Values may be sent and summed in bfloat16 or wider, within the bound.
A program may use at most 256 MiB of HBM per device.

v0:
```python
import math

import jax
import jax.numpy as jnp
from jax import lax
from jax.sharding import PartitionSpec as P

DIRS = 36
FRQS = 36


VISCOSITY = 0.1
CORIOLIS = 0.3
INPUT_SCALE = 5.0
SOURCE_STEP = 1.0
SPEED_MAX = 0.25


def with_halo(cells, sides, width):
    for axis, dim in sides:
        count = lax.axis_size(axis)
        ends = count - 1
        head = lax.slice_in_dim(cells, 0, width, axis=dim)
        tail = lax.slice_in_dim(cells, cells.shape[dim] - width, cells.shape[dim], axis=dim)
        cells = jnp.concatenate(
            [
                lax.ppermute(tail, axis, [(i, (i + 1) % count) for i in range(ends)]),
                cells,
                lax.ppermute(head, axis, [((i + 1) % count, i) for i in range(ends)]),
            ],
            axis=dim,
        )
    return cells


def bin_tables():
    index = jnp.arange(DIRS * FRQS, dtype=jnp.int32)
    heading = (index // FRQS).astype(jnp.float32)
    level = (index % FRQS).astype(jnp.float32)
    theta = (heading + 0.5) * (2.0 * math.pi / DIRS)
    speed = SPEED_MAX * jnp.exp(-math.log(1.1) * level)
    factor = 2.0 / math.sqrt(DIRS * FRQS)
    cosine = jnp.cos(theta)
    sine = jnp.sin(theta)
    speeds = jnp.stack([speed * cosine, speed * sine])
    drift_rows = jnp.stack([cosine, sine]) * (factor * (1.0 + level / FRQS))
    stress_rows = jnp.stack([cosine, sine]) * factor
    return (speeds, drift_rows, stress_rows)


def divergence(energy, speed, axis):
    count = energy.shape[axis] - 1
    lower_energy = lax.slice_in_dim(energy, 0, count, axis=axis)
    upper_energy = lax.slice_in_dim(energy, 1, count + 1, axis=axis)
    lower_speed = lax.slice_in_dim(speed, 0, count, axis=axis)
    upper_speed = lax.slice_in_dim(speed, 1, count + 1, axis=axis)
    flux = (
        jnp.maximum(lower_speed, 0.0) * lower_energy + jnp.minimum(upper_speed, 0.0) * upper_energy
    )
    return lax.slice_in_dim(flux, 1, count, axis=axis) - lax.slice_in_dim(
        flux, 0, count - 1, axis=axis
    )


def wave_step(packed, spectral_in, spectral_out, speeds):
    bins = speeds.shape[1]
    spectral = packed[:bins]
    currents = packed[bins:].astype(jnp.float32)
    inner = spectral[:, 1:-1]
    hidden = jax.nn.gelu(
        jnp.dot(spectral_in, inner.reshape(bins, -1), preferred_element_type=jnp.float32)
    ).astype(jnp.bfloat16)
    source = jnp.dot(spectral_out, hidden, preferred_element_type=jnp.float32).reshape(inner.shape)
    energy = spectral.astype(jnp.float32)
    along_x = divergence(energy, speeds[0][:, None, None] + currents[0][None], 1)
    energy_in = energy[:, 1:-1]
    pad_rows = ((0, 0), (0, 0), (1, 1))
    speed_rows = speeds[1][:, None, None] + currents[1][None, 1:-1]
    along_y = divergence(jnp.pad(energy_in, pad_rows), jnp.pad(speed_rows, pad_rows), 2)
    updated = currents[2][None, 1:-1] * (energy_in - (along_x + along_y) + SOURCE_STEP * source)
    return (updated.astype(jnp.bfloat16), source)


def conv_layer(weights, inputs):
    rows = inputs.shape[1] - 2
    width = inputs.shape[2]
    padded = jnp.pad(inputs, ((0, 0), (0, 0), (1, 1)))
    taps = [
        padded[:, 1 + row_step : 1 + row_step + rows, 1 + col_step : 1 + col_step + width]
        for row_step in (-1, 0, 1)
        for col_step in (-1, 0, 1)
    ]
    stacked = jnp.concatenate(taps, axis=0)
    total = jnp.dot(
        weights, stacked.reshape(stacked.shape[0], -1), preferred_element_type=jnp.float32
    )
    return total.reshape(weights.shape[0], rows, width)


def laplacian(fields):
    rows = fields.shape[1] - 2
    padded = jnp.pad(fields, ((0, 0), (0, 0), (1, 1)))
    center = padded[:, 1 : 1 + rows, 1:-1]
    beside_all = (
        padded[:, :rows, 1:-1]
        + padded[:, 2 : 2 + rows, 1:-1]
        + padded[:, 1 : 1 + rows, :-2]
        + padded[:, 1 : 1 + rows, 2:]
    )
    return beside_all - 4.0 * center


def local(
    east_current,
    north_current,
    land_mask,
    spectrum,
    spectral_in,
    spectral_out,
    conv_first,
    conv_second,
    conv_last,
):
    rows = east_current.shape[0]
    width = east_current.shape[1]
    bins = spectrum.shape[0]
    columns = spectrum.shape[1]
    sea = land_mask.astype(jnp.float32)
    masked = jnp.stack([east_current * sea, north_current * sea])
    outgoing = jnp.concatenate([masked, sea[None]], axis=0).astype(jnp.bfloat16).transpose(0, 2, 1)
    coupled = lax.all_to_all(outgoing, "gx", split_axis=1, concat_axis=2, tiled=True)
    speeds, drift_rows, stress_rows = bin_tables()
    state = jnp.concatenate([spectrum, coupled], axis=0)
    current_state = state
    for step_number in range(2):
        padded_state = with_halo(current_state, (("gx", 1),), 1)
        final, source = wave_step(padded_state, spectral_in, spectral_out, speeds)
        current_state = jnp.concatenate([final, coupled], axis=0)
    drift = jnp.dot(
        drift_rows, final.astype(jnp.float32).reshape(bins, -1), precision=lax.Precision.HIGHEST
    )
    stress = jnp.dot(stress_rows, source.reshape(bins, -1), precision=lax.Precision.HIGHEST)
    forcing = jnp.concatenate([drift, stress], axis=0).reshape(4, columns, spectrum.shape[2])
    returned = lax.all_to_all(forcing, "gx", split_axis=2, concat_axis=1, tiled=True)
    returned = returned.transpose(0, 2, 1)
    near_field = with_halo(masked, (("gx", 1),), 1)
    scaled = (INPUT_SCALE * near_field).astype(jnp.bfloat16)
    first_hidden = jax.nn.relu(conv_layer(conv_first, scaled)).astype(jnp.bfloat16)
    second_input = with_halo(first_hidden, (("gx", 1),), 1)
    second_hidden = jax.nn.relu(conv_layer(conv_second, second_input)).astype(jnp.bfloat16)
    closure = jnp.dot(
        conv_last,
        second_hidden.reshape(second_hidden.shape[0], -1),
        preferred_element_type=jnp.float32,
    ).reshape(2, rows, width)
    bend = laplacian(near_field)
    east_next = sea * (
        masked[0]
        + VISCOSITY * bend[0]
        + CORIOLIS * (masked[1] + returned[1])
        + returned[2]
        + closure[0]
    )
    north_next = sea * (
        masked[1]
        + VISCOSITY * bend[1]
        - CORIOLIS * (masked[0] + returned[0])
        + returned[3]
        + closure[1]
    )
    return (east_next, north_next, final)


def solution(mesh):
    in_specs = (
        P(("groups", "gx"), None),
        P(("groups", "gx"), None),
        P(("groups", "gx"), None),
        P(None, ("groups", "gx"), None),
        P(),
        P(),
        P(),
        P(),
        P(),
    )
    out_specs = (
        P(("groups", "gx"), None),
        P(("groups", "gx"), None),
        P(None, ("groups", "gx"), None),
    )
    return jax.shard_map(local, mesh=mesh, in_specs=in_specs, out_specs=out_specs, check_vma=False)
```

profile of v0, /device:TPU:0, one launch (start us, length us, event | category | flops | bytes accessed | tf_op | source)
XLA Modules:
  0.0 123.3 jit_solution(2387074925443560108)
XLA Ops:
  0.7 0.9 copy.82
  1.6 0.8 copy.83
  2.3 0.8 copy.84
  3.1 0.6 copy.85
  3.8 7.4 %all-to-all-start = ((bf16[3,32,16]{2,0,1:T(4,128)(2,1)}), bf16[3,32,16]{2,0,1:T(4,128)(2,1)}, u32[]{:S(2)}, u32[]{:S(2)}) async-start(bf16[3,32,16]{2,0,1:T(4,128)(2,1)} %copy.85), calls=%async_computation | async-start | bytes 65536 | tf_op jit(solution)/shard_map/all_to_all | solution.py:131
  11.3 2.3 %collective-permute-start = (f32[2,1,32]{1,2,0:T(8,128)S(1)}, f32[2,1,32]{1,2,0:T(8,128)S(1)}, u32[]{:S(2)}, u32[]{:S(2)}) collective-permute-start(f32[2,1,32]{1,2,0:T(8,128)S(1)} %get-tuple-element.46), channel_id=1, source_target_pairs={{0,1},{1,2},{2,3},{3,4},{4,5},{5,6},{6,7},{7,8},{8,9},{9,10},{10,1... | collective-permute-start | bytes 776 | tf_op jit(solution)/shard_map/ppermute | solution.py:27
  13.6 1.3 %collective-permute-start.1 = (f32[2,1,32]{1,2,0:T(8,128)S(1)}, f32[2,1,32]{1,2,0:T(8,128)S(1)}, u32[]{:S(2)}, u32[]{:S(2)}) collective-permute-start(f32[2,1,32]{1,2,0:T(8,128)S(1)} %get-tuple-element.47), channel_id=1, source_target_pairs={{1,0},{2,1},{3,2},{4,3},{5,4},{6,5},{7,6},{8,7},{9,8},{10,9},{11,1... | collective-permute-start | bytes 776 | tf_op jit(solution)/shard_map/ppermute | solution.py:29
  14.9 0.7 sine_multiply_fusion
  15.5 0.7 cosine_multiply_fusion
  16.2 0.8 fusion.106
  17.0 1.5 %copy_dynamic-update-slice_fusion = bf16[1299,2,256]{2,0,1:T(8,128)(2,1)S(1)} fusion(bf16[1296,2,256]{2,1,0:T(2,128)(2,1)} %param.12), kind=kLoop, calls=%fused_computation.53 | loop fusion | bytes 2654208
  18.5 1.3 %copy.120 = bf16[162,8,2,256]{3,1,2,0:T(8,128)(2,1)} copy(bf16[162,8,2,256]{3,2,1,0:T(2,128)(2,1)S(1)} %bitcast.143) | data formatting | bytes 2654208
  19.8 4.2 %fusion.46 = f32[512,1296]{0,1:T(8,128)} fusion(bf16[1296,256]{1,0:T(8,128)(2,1)S(1)} %copy-done, bf16[256,1296]{0,1:T(8,128)(2,1)} %param.13, bf16[1296,512]{1,0:T(8,128)(2,1)} %bitcast.145), kind=kOutput, calls=%fused_computation.88 | convolution fusion | flops 680656896 | bytes 5308416 | tf_op jit(solution)/shard_map/dot_general | solution.py:73
  24.0 0.6 add_multiply_fusion
  24.7 0.7 multiply_convert_fusion
  26.2 0.2 fusion.25
  26.6 0.8 copy.86
  27.5 1.2 fusion.126
  28.6 4.2 %collective-permute-start.2 = (bf16[1299,1,256]{2,0,1:T(8,128)(2,1)}, bf16[1299,1,256]{2,0,1:T(8,128)(2,1)S(1)}, u32[]{:S(2)}, u32[]{:S(2)}) collective-permute-start(bf16[1299,1,256]{2,0,1:T(8,128)(2,1)} %get-tuple-element.30), channel_id=1, source_target_pairs={{0,1},{1,2},{2,3},{3,4},{4,5},{5,6},{6,7},{7,8},{8,9},{9,10},{10,1... | collective-permute-start | bytes 1995272 | tf_op jit(solution)/shard_map/ppermute | solution.py:27
  32.8 1.3 %collective-permute-start.3 = (bf16[1299,1,256]{2,0,1:T(8,128)(2,1)}, bf16[1299,1,256]{2,0,1:T(8,128)(2,1)S(1)}, u32[]{:S(2)}, u32[]{:S(2)}) collective-permute-start(bf16[1299,1,256]{2,0,1:T(8,128)(2,1)} %get-tuple-element.31), channel_id=1, source_target_pairs={{1,0},{2,1},{3,2},{4,3},{5,4},{6,5},{7,6},{8,7},{9,8},{10,9},{11,1... | collective-permute-start | bytes 1995272 | tf_op jit(solution)/shard_map/ppermute | solution.py:29
  34.1 4.2 %collective-permute-start.6 = (bf16[64,1,32]{0,2,1:T(8,128)(2,1)S(1)}, bf16[64,1,32]{0,2,1:T(8,128)(2,1)S(1)}, u32[]{:S(2)}, u32[]{:S(2)}) collective-permute-start(bf16[64,1,32]{0,2,1:T(8,128)(2,1)S(1)} %get-tuple-element.44), channel_id=1, source_target_pairs={{0,1},{1,2},{2,3},{3,4},{4,5},{5,6},{6,7},{7,8},{8,9},{9,10},{10,1... | collective-permute-start | bytes 12296 | tf_op jit(solution)/shard_map/ppermute | solution.py:27
  38.4 1.3 %collective-permute-start.7 = (bf16[64,1,32]{0,2,1:T(8,128)(2,1)S(1)}, bf16[64,1,32]{0,2,1:T(8,128)(2,1)S(1)}, u32[]{:S(2)}, u32[]{:S(2)}) collective-permute-start(bf16[64,1,32]{0,2,1:T(8,128)(2,1)S(1)} %get-tuple-element.45), channel_id=1, source_target_pairs={{1,0},{2,1},{3,2},{4,3},{5,4},{6,5},{7,6},{8,7},{9,8},{10,9},{11,1... | collective-permute-start | bytes 12296 | tf_op jit(solution)/shard_map/ppermute | solution.py:29
  39.7 0.7 fusion.64
  40.4 2.2 %collective-permute-done.7 = bf16[64,1,32]{0,2,1:T(8,128)(2,1)S(1)} collective-permute-done((bf16[64,1,32]{0,2,1:T(8,128)(2,1)S(1)}, bf16[64,1,32]{0,2,1:T(8,128)(2,1)S(1)}, u32[]{:S(2)}, u32[]{:S(2)}) %collective-permute-start.7) | collective-permute-done | bytes 4128 | tf_op jit(solution)/shard_map/ppermute | solution.py:29
  42.8 1.0 pad_maximum_fusion.6
  43.8 2.1 %concatenate.57 = bf16[576,16,32]{0,2,1:T(8,128)(2,1)} concatenate(bf16[64,16,32]{0,2,1:T(8,128)(2,1)} %get-tuple-element.50, bf16[64,16,32]{0,2,1:T(8,128)(2,1)} %get-tuple-element.43, bf16[64,16,32]{0,2,1:T(8,128)(2,1)} %get-tuple-element.51, bf16[64,16,32]{0,2,1:T(8,128)(2,1)} %get-tuple-element.52, bf16[64,16,32]{0,2,1:T(8,128)(2,1)S(1)} %bitcast.151, ...), dimensions={0} | concatenate | bytes 1179648 | tf_op jit(solution)/shard_map/concatenate | solution.py:93
  46.0 0.4 fusion.21
  46.5 0.7 copy-done.16
  47.2 0.4 broadcast_add_fusion.1
  47.6 1.2 copy-done.2
  48.8 2.7 %fusion.11 = f32[1296,3,256]{2,0,1:T(8,128)} fusion(f32[1296,4,256]{2,0,1:T(8,128)S(1)} %fusion.21, f32[1296,4,256]{2,0,1:T(8,128)S(1)} %broadcast_add_fusion.1), kind=kLoop, calls=%fused_computation.24 | loop fusion | flops 4976640 | bytes 19906560 | tf_op jit(solution)/shard_map/add | solution.py:58
  51.5 0.7 copy-done.15
  52.2 0.2 broadcast_add_fusion.3
  52.4 0.8 slice-done.2
  53.3 3.9 %fusion.2 = f32[1296,2,257]{2,0,1:T(8,128)} fusion(f32[1296,2,256]{2,0,1:T(8,128)S(1)} %broadcast_add_fusion.3, f32[1296,2,256]{2,0,1:T(8,128)S(1)} %slice-done.2), kind=kLoop, calls=%fused_computation.10 | loop fusion | flops 3330720 | bytes 7972992 | tf_op jit(solution)/shard_map/add | solution.py:58
  57.2 5.1 %fusion.15 = bf16[1296,2,256]{2,0,1:T(8,128)(2,1)S(1)} fusion(f32[162,2,8,256]{3,2,1,0:T(8,128)} %bitcast.142, f32[1296,2,257]{2,0,1:T(8,128)} %fusion.2, f32[1296,3,256]{2,0,1:T(8,128)S(1)} %copy-done.6, f32[2,256]{1,0:T(2,128)S(1)} %get-tuple-element.57, f32[1296,4,256]{2,0,1:T(8,128)S(1)} %bitcast.138), kind=kLoop, calls=%fused_computation.33 | loop fusion | flops 4644864 | bytes 17254400 | tf_op jit(solution)/shard_map/convert_element_type | solution.py:81
  62.3 1.2 fusion.27
  63.5 9.0 %collective-permute-start.4 = (bf16[1299,1,256]{2,0,1:T(8,128)(2,1)}, bf16[1299,1,256]{2,0,1:T(8,128)(2,1)S(1)}, u32[]{:S(2)}, u32[]{:S(2)}) collective-permute-start(bf16[1299,1,256]{2,0,1:T(8,128)(2,1)} %get-tuple-element.32), channel_id=1, source_target_pairs={{0,1},{1,2},{2,3},{3,4},{4,5},{5,6},{6,7},{7,8},{8,9},{9,10},{10,1... | collective-permute-start | bytes 1995272 | tf_op jit(solution)/shard_map/ppermute | solution.py:27
  72.5 1.5 %collective-permute-start.5 = (bf16[1299,1,256]{2,0,1:T(8,128)(2,1)}, bf16[1299,1,256]{2,0,1:T(8,128)(2,1)S(1)}, u32[]{:S(2)}, u32[]{:S(2)}) collective-permute-start(bf16[1299,1,256]{2,0,1:T(8,128)(2,1)} %get-tuple-element.33), channel_id=1, source_target_pairs={{1,0},{2,1},{3,2},{4,3},{5,4},{6,5},{7,6},{8,7},{9,8},{10,9},{11,1... | collective-permute-start | bytes 1995272 | tf_op jit(solution)/shard_map/ppermute | solution.py:29
  74.0 1.5 %fusion.26 = f32[2,512]{1,0:T(2,128)S(1)} fusion(bf16[2,64]{1,0:T(2,128)(2,1)S(1)} %copy-done.21, bf16[576,512]{0,1:T(8,128)(2,1)} %bitcast.147, bf16[64,576]{1,0:T(8,128)(2,1)S(1)} %copy-done.14), kind=kOutput, calls=%fused_computation.63 | convolution fusion | flops 37945344 | bytes 667904 | tf_op jit(solution)/shard_map/dot_general | solution.py:151
  75.5 1.2 copy.118
  76.7 4.2 %fusion.44 = f32[512,1296]{0,1:T(8,128)} fusion(bf16[1296,256]{1,0:T(8,128)(2,1)S(1)} %copy-done, bf16[1296,512]{1,0:T(8,128)(2,1)} %bitcast.146, bf16[256,1296]{0,1:T(8,128)(2,1)} %param.13), kind=kOutput, calls=%fused_computation.86 | convolution fusion | flops 680656896 | bytes 5308416 | tf_op jit(solution)/shard_map/dot_general | solution.py:73
  80.9 3.1 %fusion.87 = f32[2,512]{1,0:T(2,128)S(1)} fusion(f32[512,1296]{0,1:T(8,128)} %fusion.44, f32[1,1296]{1,0:T(1,128)S(1)} %copy-done.17, f32[1,1296]{1,0:T(1,128)S(1)} %copy-done.18), kind=kOutput, calls=%fused_computation.178 | convolution fusion | flops 15930432 | bytes 2668672 | tf_op jit(solution)/shard_map/dot_general | solution.py:142
  84.1 0.4 broadcast_add_fusion
  84.5 0.4 fusion.18
  85.0 3.1 %fusion.10 = f32[1296,3,256]{2,0,1:T(8,128)} fusion(f32[1296,4,256]{2,0,1:T(8,128)S(1)} %fusion.18, f32[1296,4,256]{2,0,1:T(8,128)S(1)} %broadcast_add_fusion), kind=kLoop, calls=%fused_computation.19 | loop fusion | flops 4976640 | bytes 19906560 | tf_op jit(solution)/shard_map/add | solution.py:58
  88.0 0.5 copy-done.3
  88.6 0.2 broadcast_add_fusion.2
  88.9 1.5 %slice-done.3 = f32[1296,2,256]{2,0,1:T(8,128)S(1)} async-done(((f32[1296,4,256]{2,0,1:T(8,128)}), f32[1296,2,256]{2,0,1:T(8,128)S(1)}, s32[]{:S(2)}) %slice-start.3) | async-done | bytes 2654232 | tf_op jit(solution)/shard_map/slice | solution.py:76
  90.3 2.5 %fusion.7 = f32[1296,2,257]{2,0,1:T(8,128)S(1)} fusion(f32[1296,2,256]{2,0,1:T(8,128)S(1)} %broadcast_add_fusion.2, f32[1296,2,256]{2,0,1:T(8,128)S(1)} %slice-done.3), kind=kLoop, calls=%fused_computation.15 | loop fusion | flops 3330720 | bytes 7972992 | tf_op jit(solution)/shard_map/add | solution.py:58
  92.9 0.8 copy-done.5
  93.7 4.0 %fusion.13 = bf16[1296,2,256]{2,0,1:T(8,128)(2,1)S(1)} fusion(f32[162,2,8,256]{3,2,1,0:T(8,128)S(1)} %bitcast.140, f32[1296,2,257]{2,0,1:T(8,128)S(1)} %fusion.7, f32[1296,3,256]{2,0,1:T(8,128)} %fusion.10, f32[2,256]{1,0:T(2,128)S(1)} %bitcast.160, f32[1296,4,256]{2,0,1:T(8,128)S(1)} %copy-done.4), kind=kLoop, calls=%fused_computation.30 | loop fusion | flops 4644864 | bytes 17254400 | tf_op jit(solution)/shard_map/convert_element_type | solution.py:81
  97.8 0.6 copy-done.19
  98.3 0.6 fusion.89
  99.0 0.2 copy.96
  99.2 1.0 reshape.164
  100.1 11.5 %all-to-all-start.1 = ((f32[16,1,128]{2,1,0:T(1,128)}), f32[16,1,128]{2,1,0:T(1,128)S(1)}, u32[]{:S(2)}, u32[]{:S(2)}) async-start(f32[16,1,128]{2,1,0:T(1,128)} %reshape.164), calls=%async_computation.1 | async-start | bytes 16384 | tf_op jit(solution)/shard_map/all_to_all | solution.py:144
  112.0 8.0 %copy.95 = bf16[1296,2,256]{2,1,0:T(2,128)(2,1)} copy(bf16[1296,2,256]{2,0,1:T(8,128)(2,1)S(1)} %fusion.13) | data formatting | bytes 2654208 | tf_op jit(solution)/shard_map/convert_element_type | solution.py:81
  120.0 0.5 broadcast.302
  120.5 0.7 reduce.8
  121.1 0.4 reshape.165
  121.6 0.3 copy.107
  122.0 0.7 copy.103
  122.6 0.7 copy.104
  (94 shorter events, 1.9 us)
Async XLA Ops:
  0.6 19.2 %copy-start = (bf16[1296,256]{1,0:T(8,128)(2,1)S(1)}, bf16[1296,256]{1,0:T(8,128)(2,1)}, u32[]{:S(2)}) copy-start(bf16[1296,256]{1,0:T(8,128)(2,1)} %param.14) | copy-start | bytes 1990660
  0.6 17.8 %copy-start.7 = (bf16[1296,2,256]{2,1,0:T(2,128)(2,1)S(1)}, bf16[1296,2,256]{2,1,0:T(2,128)(2,1)}, u32[]{:S(2)}) copy-start(bf16[1296,2,256]{2,1,0:T(2,128)(2,1)} %param.12) | copy-start | bytes 3981316
  3.8 22.8 %all-to-all-start = ((bf16[3,32,16]{2,0,1:T(4,128)(2,1)}), bf16[3,32,16]{2,0,1:T(4,128)(2,1)}, u32[]{:S(2)}, u32[]{:S(2)}) async-start(bf16[3,32,16]{2,0,1:T(4,128)(2,1)} %copy.85), calls=%async_computation | async-start | bytes 65536 | tf_op jit(solution)/shard_map/all_to_all | solution.py:131
  11.3 13.3 %collective-permute-start = (f32[2,1,32]{1,2,0:T(8,128)S(1)}, f32[2,1,32]{1,2,0:T(8,128)S(1)}, u32[]{:S(2)}, u32[]{:S(2)}) collective-permute-start(f32[2,1,32]{1,2,0:T(8,128)S(1)} %get-tuple-element.46), channel_id=1, source_target_pairs={{0,1},{1,2},{2,3},{3,4},{4,5},{5,6},{6,7},{7,8},{8,9},{9,10},{10,1... | collective-permute-start | bytes 776 | tf_op jit(solution)/shard_map/ppermute | solution.py:27
  13.6 11.1 %collective-permute-start.1 = (f32[2,1,32]{1,2,0:T(8,128)S(1)}, f32[2,1,32]{1,2,0:T(8,128)S(1)}, u32[]{:S(2)}, u32[]{:S(2)}) collective-permute-start(f32[2,1,32]{1,2,0:T(8,128)S(1)} %get-tuple-element.47), channel_id=1, source_target_pairs={{1,0},{2,1},{3,2},{4,3},{5,4},{6,5},{7,6},{8,7},{9,8},{10,9},{11,1... | collective-permute-start | bytes 776 | tf_op jit(solution)/shard_map/ppermute | solution.py:29
  19.8 6.4 %copy-start.20 = (bf16[64,18]{0,1:T(8,128)(2,1)S(1)}, bf16[64,18]{0,1:T(8,128)(2,1)}, u32[]{:S(2)}) copy-start(bf16[64,18]{0,1:T(8,128)(2,1)} %param.15) | copy-start | bytes 6916
  24.6 1.5 %copy-start.9 = (f32[2,1,32]{1,2,0:T(8,128)}, f32[2,1,32]{1,2,0:T(8,128)S(1)}, u32[]{:S(2)}) copy-start(f32[2,1,32]{1,2,0:T(8,128)S(1)} %collective-permute-done) | copy-start | bytes 772
  24.6 1.5 %copy-start.11 = (f32[2,1,32]{1,2,0:T(8,128)}, f32[2,1,32]{1,2,0:T(8,128)S(1)}, u32[]{:S(2)}) copy-start(f32[2,1,32]{1,2,0:T(8,128)S(1)} %collective-permute-done.1) | copy-start | bytes 772
  27.4 12.2 %copy-start.10 = (f32[2,1,32]{1,2,0:T(8,128)S(1)}, f32[2,1,32]{1,2,0:T(8,128)}, u32[]{:S(2)}) copy-start(f32[2,1,32]{1,2,0:T(8,128)} %copy-done.9) | copy-start | bytes 772
  27.4 12.2 %copy-start.12 = (f32[2,1,32]{1,2,0:T(8,128)S(1)}, f32[2,1,32]{1,2,0:T(8,128)}, u32[]{:S(2)}) copy-start(f32[2,1,32]{1,2,0:T(8,128)} %copy-done.11) | copy-start | bytes 772
  27.4 12.2 %copy-start.13 = (f32[2,18,32]{1,2,0:T(8,128)S(1)}, f32[2,18,32]{1,2,0:T(8,128)}, u32[]{:S(2)}) copy-start(f32[2,18,32]{1,2,0:T(8,128)} %get-tuple-element.25) | copy-start | bytes 13828
  28.6 17.3 %collective-permute-start.2 = (bf16[1299,1,256]{2,0,1:T(8,128)(2,1)}, bf16[1299,1,256]{2,0,1:T(8,128)(2,1)S(1)}, u32[]{:S(2)}, u32[]{:S(2)}) collective-permute-start(bf16[1299,1,256]{2,0,1:T(8,128)(2,1)} %get-tuple-element.30), channel_id=1, source_target_pairs={{0,1},{1,2},{2,3},{3,4},{4,5},{5,6},{6,7},{7,8},{8,9},{9,10},{10,1... | collective-permute-start | bytes 1995272 | tf_op jit(solution)/shard_map/ppermute | solution.py:27
  32.8 13.1 %collective-permute-start.3 = (bf16[1299,1,256]{2,0,1:T(8,128)(2,1)}, bf16[1299,1,256]{2,0,1:T(8,128)(2,1)S(1)}, u32[]{:S(2)}, u32[]{:S(2)}) collective-permute-start(bf16[1299,1,256]{2,0,1:T(8,128)(2,1)} %get-tuple-element.31), channel_id=1, source_target_pairs={{1,0},{2,1},{3,2},{4,3},{5,4},{6,5},{7,6},{8,7},{9,8},{10,9},{11,1... | collective-permute-start | bytes 1995272 | tf_op jit(solution)/shard_map/ppermute | solution.py:29
  34.1 6.3 %collective-permute-start.6 = (bf16[64,1,32]{0,2,1:T(8,128)(2,1)S(1)}, bf16[64,1,32]{0,2,1:T(8,128)(2,1)S(1)}, u32[]{:S(2)}, u32[]{:S(2)}) collective-permute-start(bf16[64,1,32]{0,2,1:T(8,128)(2,1)S(1)} %get-tuple-element.44), channel_id=1, source_target_pairs={{0,1},{1,2},{2,3},{3,4},{4,5},{5,6},{6,7},{7,8},{8,9},{9,10},{10,1... | collective-permute-start | bytes 12296 | tf_op jit(solution)/shard_map/ppermute | solution.py:27
  38.4 4.3 %collective-permute-start.7 = (bf16[64,1,32]{0,2,1:T(8,128)(2,1)S(1)}, bf16[64,1,32]{0,2,1:T(8,128)(2,1)S(1)}, u32[]{:S(2)}, u32[]{:S(2)}) collective-permute-start(bf16[64,1,32]{0,2,1:T(8,128)(2,1)S(1)} %get-tuple-element.45), channel_id=1, source_target_pairs={{1,0},{2,1},{3,2},{4,3},{5,4},{6,5},{7,6},{8,7},{9,8},{10,9},{11,1... | collective-permute-start | bytes 12296 | tf_op jit(solution)/shard_map/ppermute | solution.py:29
  46.4 2.4 %copy-start.2 = (f32[1296,4,256]{2,0,1:T(8,128)}, f32[1296,4,256]{2,0,1:T(8,128)S(1)}, u32[]{:S(2)}) copy-start(f32[1296,4,256]{2,0,1:T(8,128)S(1)} %fusion.21) | copy-start | bytes 15925252
  46.4 0.7 copy-start.16
  51.5 0.7 copy-start.15
  51.5 1.8 %slice-start.2 = ((f32[1296,4,256]{2,0,1:T(8,128)}), f32[1296,2,256]{2,0,1:T(8,128)S(1)}, s32[]{:S(2)}) async-start(f32[1296,4,256]{2,0,1:T(8,128)} %copy-done.2), calls=%async_computation.4 | async-start | bytes 5308416 | tf_op jit(solution)/shard_map/slice | solution.py:76
  52.2 5.0 %slice-start = ((s8[5308416]{0:T(1024)(128)(4,1)}), s8[4194304]{0:T(1024)(128)(4,1)S(1)}, s32[]{:S(2)}) async-start(s8[5308416]{0:T(1024)(128)(4,1)} %bitcast.137), calls=%async_computation.2 | async-start | bytes 8388608
  53.3 3.9 %slice-start.1 = ((s8[5308416]{0:T(1024)(128)(4,1)}), s8[1114112]{0:T(1024)(128)(4,1)S(1)}, s32[]{:S(2)}) async-start(s8[5308416]{0:T(1024)(128)(4,1)} %bitcast.137), calls=%async_computation.3 | async-start | bytes 2228224
  53.3 3.9 %copy-start.6 = (f32[1296,3,256]{2,0,1:T(8,128)S(1)}, f32[1296,3,256]{2,0,1:T(8,128)}, u32[]{:S(2)}) copy-start(f32[1296,3,256]{2,0,1:T(8,128)} %fusion.11) | copy-start | bytes 11943940
  62.3 11.7 %copy-start.14 = (bf16[64,576]{1,0:T(8,128)(2,1)S(1)}, bf16[64,576]{1,0:T(8,128)(2,1)}, u32[]{:S(2)}) copy-start(bf16[64,576]{1,0:T(8,128)(2,1)} %param.16) | copy-start | bytes 221188
  62.3 11.7 %copy-start.21 = (bf16[2,64]{1,0:T(2,128)(2,1)S(1)}, bf16[2,64]{1,0:T(2,128)(2,1)}, u32[]{:S(2)}) copy-start(bf16[2,64]{1,0:T(2,128)(2,1)} %param.17) | copy-start | bytes 772
  63.5 20.5 %collective-permute-start.4 = (bf16[1299,1,256]{2,0,1:T(8,128)(2,1)}, bf16[1299,1,256]{2,0,1:T(8,128)(2,1)S(1)}, u32[]{:S(2)}, u32[]{:S(2)}) collective-permute-start(bf16[1299,1,256]{2,0,1:T(8,128)(2,1)} %get-tuple-element.32), channel_id=1, source_target_pairs={{0,1},{1,2},{2,3},{3,4},{4,5},{5,6},{6,7},{7,8},{8,9},{9,10},{10,1... | collective-permute-start | bytes 1995272 | tf_op jit(solution)/shard_map/ppermute | solution.py:27
  72.5 11.5 %collective-permute-start.5 = (bf16[1299,1,256]{2,0,1:T(8,128)(2,1)}, bf16[1299,1,256]{2,0,1:T(8,128)(2,1)S(1)}, u32[]{:S(2)}, u32[]{:S(2)}) collective-permute-start(bf16[1299,1,256]{2,0,1:T(8,128)(2,1)} %get-tuple-element.33), channel_id=1, source_target_pairs={{1,0},{2,1},{3,2},{4,3},{5,4},{6,5},{7,6},{8,7},{9,8},{10,9},{11,1... | collective-permute-start | bytes 1995272 | tf_op jit(solution)/shard_map/ppermute | solution.py:29
  76.7 4.2 %copy-start.17 = (f32[1,1296]{1,0:T(1,128)S(1)}, f32[1,1296]{1,0:T(1,128)}, u32[]{:S(2)}) copy-start(f32[1,1296]{1,0:T(1,128)} %get-tuple-element.58) | copy-start | bytes 15556
  76.7 4.2 %copy-start.18 = (f32[1,1296]{1,0:T(1,128)S(1)}, f32[1,1296]{1,0:T(1,128)}, u32[]{:S(2)}) copy-start(f32[1,1296]{1,0:T(1,128)} %get-tuple-element.59) | copy-start | bytes 15556
  85.0 3.6 %copy-start.3 = (f32[1296,4,256]{2,0,1:T(8,128)}, f32[1296,4,256]{2,0,1:T(8,128)S(1)}, u32[]{:S(2)}) copy-start(f32[1296,4,256]{2,0,1:T(8,128)S(1)} %fusion.18) | copy-start | bytes 15925252
  88.6 1.7 %slice-start.3 = ((f32[1296,4,256]{2,0,1:T(8,128)}), f32[1296,2,256]{2,0,1:T(8,128)S(1)}, s32[]{:S(2)}) async-start(f32[1296,4,256]{2,0,1:T(8,128)} %copy-done.3), calls=%async_computation.5 | async-start | bytes 5308416 | tf_op jit(solution)/shard_map/slice | solution.py:76
  90.3 2.6 %copy-start.4 = (f32[1296,4,256]{2,0,1:T(8,128)S(1)}, f32[1296,4,256]{2,0,1:T(8,128)}, u32[]{:S(2)}) copy-start(f32[1296,4,256]{2,0,1:T(8,128)} %copy-done.3) | copy-start | bytes 15925252
  90.3 3.3 %copy-start.5 = (f32[512,1296]{0,1:T(8,128)S(1)}, f32[512,1296]{0,1:T(8,128)}, u32[]{:S(2)}) copy-start(f32[512,1296]{0,1:T(8,128)} %fusion.44) | copy-start | bytes 7962628
  97.6 0.7 copy-start.19
  97.8 25.5 %copy-start.1 = (bf16[1296,256]{1,0:T(8,128)(2,1)S(1)}, bf16[1296,256]{1,0:T(8,128)(2,1)}, u32[]{:S(2)}) copy-start(bf16[1296,256]{1,0:T(8,128)(2,1)} %param.14) | copy-start | bytes 1990660
  98.3 23.6 %copy-start.8 = (f32[2,16,32]{1,2,0:T(8,128)S(1)}, f32[2,16,32]{1,2,0:T(8,128)}, u32[]{:S(2)}) copy-start(f32[2,16,32]{1,2,0:T(8,128)} %fusion.64) | copy-start | bytes 12292
  100.1 19.8 %all-to-all-start.1 = ((f32[16,1,128]{2,1,0:T(1,128)}), f32[16,1,128]{2,1,0:T(1,128)S(1)}, u32[]{:S(2)}, u32[]{:S(2)}) async-start(f32[16,1,128]{2,1,0:T(1,128)} %reshape.164), calls=%async_computation.1 | async-start | bytes 16384 | tf_op jit(solution)/shard_map/all_to_all | solution.py:144
where the time goes:
time: 124 us; the launch traced here: 123 us
  starting transfers between devices  43.9 us (35%)
  local copies, waits for them, and re-layouts  31.3 us (25%)
  other arithmetic  30.7 us (25%)
  matrix products  13.9 us (11%)
  waiting for transfers between devices  2.27 us (2%)
    ppermute x4, starting transfers between devices, with_halo(): lax.ppermute(tail, axis, [(i, (i + 1) % count) for i in range(ends)])  19.7 us
    unnamed x70, local copies, waits for them, and re-layouts  13 us
    add x4, other arithmetic, divergence(): jnp.maximum(lower_speed, 0.0) * lower_energy  12.2 us
    all_to_all x1, starting transfers between devices, local(): lax.all_to_all(forcing, 'gx', split_axis=2, concat_axis=1, tiled=True)  11.5 us
    convert_element_type x2, other arithmetic, wave_step(): return (updated.astype(jnp.bfloat16), source)  9.04 us
    dot_general x2, matrix products, wave_step(): jnp.dot(spectral_out, hidden, preferred_element_type=jnp.float32)  8.42 us
    convert_element_type x1, local copies, waits for them, and re-layouts, wave_step(): return (updated.astype(jnp.bfloat16), source)  7.99 us
    all_to_all x1, starting transfers between devices, local(): lax.all_to_all(outgoing, 'gx', split_axis=1, concat_axis=2, tiled=True)  7.44 us
  transfers between devices with their start and end apart: 10, of which 1 were waited for; matrix products, arithmetic and copies ran while one was open for 28% of the time, Pallas kernels for 0%

commit v1 on v0

v1 whole, which is shorter than its diff:
```python
import functools
import math

import jax
import jax.numpy as jnp
import ml_dtypes
import numpy as np
from jax import lax
from jax.experimental import pallas as pl
from jax.experimental.pallas import tpu as pltpu
from jax.sharding import PartitionSpec as P

DIRS = 36
FRQS = 36
BINS = DIRS * FRQS
VISCOSITY = 0.1
CORIOLIS = 0.3
INPUT_SCALE = 5.0
SOURCE_STEP = 1.0
SPEED_MAX = 0.25

CHUNKS = 9
CHUNK = BINS // CHUNKS
BLOCK = 16
LANES = 128
MESH = pl.DeviceIdType.MESH
F32 = jnp.float32
BF16 = jnp.bfloat16
HIGHEST = lax.Precision.HIGHEST


def split_rows(row):
    pieces = []
    rest = row.astype(np.float32)
    for _ in range(3):
        piece = rest.astype(ml_dtypes.bfloat16)
        pieces.append(piece)
        rest = rest - piece.astype(np.float32)
    return pieces


def bin_tables():
    index = np.arange(BINS)
    heading = (index // FRQS).astype(np.float64)
    level = (index % FRQS).astype(np.float64)
    theta = (heading + 0.5) * (2.0 * math.pi / DIRS)
    speed = SPEED_MAX * np.exp(-math.log(1.1) * level)
    factor = 2.0 / math.sqrt(BINS)
    cosine, sine = np.cos(theta), np.sin(theta)
    speeds = np.stack([speed * cosine, speed * sine], axis=1).astype(np.float32)
    weight = factor * (1.0 + level / FRQS)
    drift = np.zeros((16, BINS), ml_dtypes.bfloat16)
    drift[0:3] = split_rows(cosine * weight)
    drift[3:6] = split_rows(sine * weight)
    stress = np.zeros((16, BINS), ml_dtypes.bfloat16)
    stress[0:3] = split_rows(cosine * factor)
    stress[3:6] = split_rows(sine * factor)
    drift = np.ascontiguousarray(drift.reshape(16, CHUNKS, CHUNK).transpose(1, 0, 2))
    return speeds, drift, stress


def iota(shape, dim):
    return lax.broadcasted_iota(jnp.int32, shape, dim)


def dot(a, b, dims=((1,), (0,)), precision=None):
    return lax.dot_general(
        a, b, (dims, ((), ())), precision=precision, preferred_element_type=F32
    )


def ones_where(cond, dtype=F32):
    return jnp.where(cond, 1.0, 0.0).astype(dtype)


def kernel(
    n,
    east_ref,
    north_ref,
    land_ref,
    energy_ref,
    win_ref,
    wout_ref,
    conv1_ref,
    conv2_ref,
    conv3_ref,
    speeds_ref,
    drift_ref,
    stress_ref,
    east_out,
    north_out,
    final_ref,
    first_ref,
    left_ref,
    right_ref,
    source_ref,
    hidden_ref,
    acc_ref,
    cur_ref,
    send_cur,
    recv_cur,
    send_for,
    recv_for,
    own_ref,
    up_ref,
    down_ref,
    taps1,
    taps2,
    drift_acc,
    drift_in,
    halo_send,
    halo_recv,
    cur_send_sem,
    cur_recv_sem,
    for_send_sem,
    for_recv_sem,
    ocean_send_sem,
    ocean_recv_sem,
):
    me = lax.axis_index("gx")
    has_left = me > 0
    has_right = me < n - 1
    rows, width = east_ref.shape
    wide = own_ref.shape[2]
    cells = cur_ref.shape[1]
    per_tile = LANES // rows
    tiles = cells // LANES

    barrier = pltpu.get_barrier_semaphore()

    @pl.loop(1, n)
    def _(d):
        peer = lax.rem(me + d, n)
        pl.semaphore_signal(barrier, inc=1, device_id={"gx": peer}, device_id_type=MESH)

    sea = land_ref[...].astype(F32)
    mu = east_ref[...] * sea
    mv = north_ref[...] * sea
    col = iota((width, 8 * n), 0)
    slot = iota((width, 8 * n), 1)
    peer_of = slot >> 3
    item = slot & 7
    pick_u = ones_where((item < 4) & (col == 2 * peer_of - 1 + item), BF16)
    pick_v = ones_where((item >= 4) & (item < 6) & (col == 2 * peer_of + item - 4), BF16)
    pick_m = ones_where((item >= 6) & (col == 2 * peer_of + item - 6), BF16)
    picked = (
        dot(mu.astype(BF16), pick_u) + dot(mv.astype(BF16), pick_v) + dot(sea.astype(BF16), pick_m)
    ).astype(BF16)
    offset = lax.rem(me * rows, LANES)
    place = iota((rows, LANES), 1) == iota((rows, LANES), 0) + offset
    blocks = dot(picked, ones_where(place, BF16), ((0,), (0,)))
    send_cur[...] = blocks.reshape(n, 8, LANES)
    recv_cur[pl.ds(me, 1)] = send_cur[pl.ds(me, 1)]
    own_ref[...] = jnp.zeros_like(own_ref)
    own_ref[0, :, :width] = mu
    own_ref[1, :, :width] = mv

    @pl.when(jnp.logical_not(has_left))
    def _():
        left_ref[...] = jnp.zeros_like(left_ref)
        up_ref[...] = jnp.zeros_like(up_ref)

    @pl.when(jnp.logical_not(has_right))
    def _():
        right_ref[...] = jnp.zeros_like(right_ref)
        down_ref[...] = jnp.zeros_like(down_ref)

    pl.semaphore_wait(barrier, n - 1)

    def current_copy(peer, d, sender):
        return pltpu.make_async_remote_copy(
            src_ref=send_cur.at[peer],
            dst_ref=recv_cur.at[sender],
            send_sem=cur_send_sem.at[d],
            recv_sem=cur_recv_sem.at[sender],
            device_id={"gx": peer},
            device_id_type=MESH,
        )

    def halo_copy(step, source, k, rightward):
        span = pl.ds(pl.multiple_of(k * CHUNK, CHUNK), CHUNK)
        side = 0 if rightward else 1
        target = left_ref if rightward else right_ref
        peer = lax.rem(me + 1, n) if rightward else lax.rem(me + n - 1, n)
        return pltpu.make_async_remote_copy(
            src_ref=source.at[1 if rightward else 0, span],
            dst_ref=target.at[step, span],
            send_sem=halo_send.at[step, side, k],
            recv_sem=halo_recv.at[step, side, k],
            device_id={"gx": peer},
            device_id_type=MESH,
        )

    def ocean_copy(downward):
        peer = lax.rem(me + 1, n) if downward else lax.rem(me + n - 1, n)
        side = 0 if downward else 1
        return pltpu.make_async_remote_copy(
            src_ref=own_ref.at[:, pl.ds(rows - 8 if downward else 0, 8)],
            dst_ref=up_ref if downward else down_ref,
            send_sem=ocean_send_sem.at[side],
            recv_sem=ocean_recv_sem.at[side],
            device_id={"gx": peer},
            device_id_type=MESH,
        )

    def forcing_copy(peer, d, sender):
        return pltpu.make_async_remote_copy(
            src_ref=send_for.at[lax.div(peer * rows, LANES)],
            dst_ref=recv_for.at[sender],
            send_sem=for_send_sem.at[d],
            recv_sem=for_recv_sem.at[sender],
            device_id={"gx": peer},
            device_id_type=MESH,
        )

    def send_halo(step, source, k):
        @pl.when(has_right)
        def _():
            halo_copy(step, source, k, True).start()

        @pl.when(has_left)
        def _():
            halo_copy(step, source, k, False).start()

    send_halo(0, energy_ref, 0)

    @pl.loop(1, n)
    def _(d):
        current_copy(lax.rem(me + d, n), d, me).start()

    @pl.when(has_right)
    def _():
        ocean_copy(True).start()

    @pl.when(has_left)
    def _():
        ocean_copy(False).start()

    @pl.loop(1, CHUNKS)
    def _(k):
        send_halo(0, energy_ref, k)

    for c in range(2):
        z = dot(win_ref[...], energy_ref[c], ((0,), (0,)))
        hidden_ref[0, c] = jax.nn.gelu(z).astype(BF16)
    acc_ref[...] = jnp.zeros_like(acc_ref)

    @pl.when(has_left)
    def _():
        ocean_copy(True).wait_recv()

    @pl.when(has_right)
    def _():
        ocean_copy(False).wait_recv()

    strip = rows + 8
    flat = strip * width
    lane = iota((wide, flat), 1)
    spread = ones_where((lane & (width - 1)) == iota((wide, flat), 0), BF16)
    ext_rows = rows + 16
    start = (iota((ext_rows, flat), 0) - 4) * width
    ahead = iota((ext_rows, flat), 1) - start
    chosen = (ahead >= 0) & (ahead < width)
    bends = []
    lines = []
    ext_r = iota((rows, ext_rows), 1)
    ext_c = iota((rows, ext_rows), 0)
    vertical = ones_where((ext_r == ext_c + 7) | (ext_r == ext_c + 9))
    side_r = iota((wide, wide), 0)
    side_c = iota((wide, wide), 1)
    horizontal = ones_where(
        ((side_r == side_c + 1) | (side_r == side_c - 1)) & (side_r < width) & (side_c < width)
    )
    for f in range(2):
        own = own_ref[f]
        ext = jnp.concatenate([up_ref[f], own, down_ref[f]], axis=0)
        line = dot((INPUT_SCALE * ext).astype(BF16), spread)
        lines.append(jnp.sum(jnp.where(chosen, line, 0.0), axis=0, keepdims=True))
        bends.append(
            dot(vertical, ext, precision=HIGHEST)
            + dot(own, horizontal, precision=HIGHEST)
            - 4.0 * own
        )
    sub = iota((8, flat), 0)
    line8 = jnp.where(sub == 0, lines[0], jnp.where(sub == 1, lines[1], 0.0))

    def shifted(x, dy, dx):
        shape = x.shape
        moved = dy * width + dx
        y = pltpu.roll(x, (-moved) % flat, 1) if moved else x
        if dx:
            at = (iota(shape, 1) & (width - 1)) + dx
            y = jnp.where((at >= 0) & (at < width), y, 0.0)
        return y

    taps = [(dy, dx) for dy in (-1, 0, 1) for dx in (-1, 0, 1)]
    for t, (dy, dx) in enumerate(taps):
        taps1[2 * t : 2 * t + 2] = shifted(line8, dy, dx)[0:2]
    h1 = dot(conv1_ref[...], taps1[0:18].astype(BF16), ((0,), (0,)))
    h1 = jnp.maximum(h1, 0.0).astype(BF16).astype(F32)
    at = iota(h1.shape, 1) + (me * rows - 4) * width
    h1 = jnp.where((at >= 0) & (at < n * rows * width), h1, 0.0)
    hc = h1.shape[0]
    for t, (dy, dx) in enumerate(taps):
        moved = shifted(h1, dy, dx)[:, 4 * width : (4 + rows) * width]
        taps2[hc * t : hc * t + hc] = moved.astype(BF16)
    h2 = jnp.maximum(dot(conv2_ref[...], taps2[...]), 0.0).astype(BF16)
    closure = dot(conv3_ref[...], h2)
    body = rows * width
    back = iota((body, wide), 0)
    gather = ones_where((back & (width - 1)) == iota((body, wide), 1))
    begun = iota((rows, body), 1) - iota((rows, body), 0) * width
    mine = (begun >= 0) & (begun < width)
    closures = [
        dot(jnp.where(mine, closure[f : f + 1], 0.0), gather, precision=HIGHEST) for f in range(2)
    ]
    mu_w, mv_w = own_ref[0], own_ref[1]
    east_part = mu_w + VISCOSITY * bends[0] + CORIOLIS * mv_w + closures[0]
    north_part = mv_w + VISCOSITY * bends[1] - CORIOLIS * mu_w + closures[1]
    east_out[...] = east_part[:, :width]
    north_out[...] = north_part[:, :width]

    @pl.loop(1, n)
    def _(d):
        sender = lax.rem(me + d, n)
        current_copy(me, d, sender).wait_recv()

    for t in range(tiles):
        cur_ref[:, t * LANES : (t + 1) * LANES] = jnp.sum(
            recv_cur[t * per_tile : (t + 1) * per_tile], axis=0
        )

    drift_acc[...] = jnp.zeros_like(drift_acc)

    def wave_chunk(step, source, target, k):
        base = pl.multiple_of(k * CHUNK, CHUNK)
        span = pl.ds(base, CHUNK)
        for c in range(2):
            source_ref[c] = dot(wout_ref[span], hidden_ref[step, c])

        @pl.when(has_left)
        def _():
            halo_copy(step, source, k, True).wait_recv()

        @pl.when(has_right)
        def _():
            halo_copy(step, source, k, False).wait_recv()

        first_lane = iota((BLOCK, cells), 1) == 0
        last_lane = iota((BLOCK, cells), 1) == cells - 1
        for i in range(CHUNK // BLOCK):
            part = pl.ds(pl.multiple_of(base + i * BLOCK, BLOCK), BLOCK)
            cx = speeds_ref[part, 0:1]
            cy = speeds_ref[part, 1:2]
            e = [
                left_ref[step, part].astype(F32),
                source[0, part].astype(F32),
                source[1, part].astype(F32),
                right_ref[step, part].astype(F32),
            ]
            s = [cx + cur_ref[q : q + 1] for q in range(4)]
            news = []
            for c in range(2):
                mid = e[c + 1]
                sy = cy + cur_ref[4 + c : 5 + c]
                ahead_flux = jnp.maximum(sy, 0.0) * mid
                back_flux = jnp.minimum(sy, 0.0) * mid
                from_before = jnp.where(first_lane, 0.0, pltpu.roll(ahead_flux, 1, 1))
                from_after = jnp.where(last_lane, 0.0, pltpu.roll(back_flux, cells - 1, 1))
                total = (
                    mid * (1.0 - jnp.abs(s[c + 1]) - jnp.abs(sy))
                    + jnp.maximum(s[c], 0.0) * e[c]
                    - jnp.minimum(s[c + 2], 0.0) * e[c + 2]
                    + from_before
                    - from_after
                    + SOURCE_STEP * source_ref[c, i * BLOCK : (i + 1) * BLOCK]
                )
                news.append(cur_ref[6 + c : 7 + c] * total)
            for c in range(2):
                if step == 0:
                    target[c, part] = news[c].astype(BF16)
                else:
                    drift_in[c, i * BLOCK : (i + 1) * BLOCK] = news[c].astype(BF16)
            if step == 1:
                target[part] = jnp.stack(news, axis=1).astype(BF16)

    @pl.loop(0, CHUNKS)
    def _(k):
        wave_chunk(0, energy_ref, first_ref, k)
        send_halo(1, first_ref, k)
        span = pl.ds(pl.multiple_of(k * CHUNK, CHUNK), CHUNK)
        for c in range(2):
            acc_ref[c] += dot(win_ref[span], first_ref[c, span], ((0,), (0,)))

    stress_rows = dot(stress_ref[...], wout_ref[...])
    stress_x = stress_rows[0:1] + stress_rows[1:2] + stress_rows[2:3]
    stress_y = stress_rows[3:4] + stress_rows[4:5] + stress_rows[5:6]
    sub8 = iota((8, stress_rows.shape[1]), 0)
    stress8 = jnp.where(sub8 == 0, stress_x, jnp.where(sub8 == 1, stress_y, 0.0))
    stresses = []
    for c in range(2):
        hidden = jax.nn.gelu(acc_ref[c]).astype(BF16)
        hidden_ref[1, c] = hidden
        stresses.append(dot(stress8, hidden.astype(F32), precision=HIGHEST))

    @pl.loop(0, CHUNKS)
    def _(k):
        wave_chunk(1, first_ref, final_ref, k)
        for c in range(2):
            drift_acc[c] += dot(drift_ref[k], drift_in[c])

    sub_f = iota((8, cells), 0)
    packed = jnp.zeros((8, cells), F32)
    for c in range(2):
        d = drift_acc[c]
        drift_x = d[0:1] + d[1:2] + d[2:3]
        drift_y = d[3:4] + d[4:5] + d[5:6]
        east_force = CORIOLIS * drift_y + stresses[c][0:1]
        north_force = stresses[c][1:2] - CORIOLIS * drift_x
        packed = jnp.where(sub_f == c, east_force, packed)
        packed = jnp.where(sub_f == 2 + c, north_force, packed)
    for t in range(tiles):
        send_for[t] = packed[:, t * LANES : (t + 1) * LANES]

    @pl.loop(1, n)
    def _(d):
        forcing_copy(lax.rem(me + d, n), d, me).start()

    recv_for[pl.ds(me, 1)] = send_for[pl.ds(lax.div(me * rows, LANES), 1)]

    @pl.loop(1, n)
    def _(d):
        current_copy(lax.rem(me + d, n), d, me).wait_send()

    @pl.when(has_right)
    def _():
        ocean_copy(True).wait_send()

    @pl.when(has_left)
    def _():
        ocean_copy(False).wait_send()

    @pl.loop(0, CHUNKS)
    def _(k):
        for step, source in ((0, energy_ref), (1, first_ref)):

            @pl.when(has_right)
            def _(step=step, source=source):
                halo_copy(step, source, k, True).wait_send()

            @pl.when(has_left)
            def _(step=step, source=source):
                halo_copy(step, source, k, False).wait_send()

    @pl.loop(1, n)
    def _(d):
        sender = lax.rem(me + d, n)
        forcing_copy(me, d, sender).wait_recv()

    arrived = recv_for[...].reshape(8 * n, LANES)
    lanes_to_rows = dot(ones_where(place), arrived, ((1,), (1,)), precision=HIGHEST)
    slot_r = iota((8 * n, width), 0)
    owner = slot_r >> 3
    which = slot_r & 7
    out_col = iota((8 * n, width), 1)
    east_pick = ones_where((which < 2) & (out_col == 2 * owner + which))
    north_pick = ones_where((which >= 2) & (which < 4) & (out_col == 2 * owner + which - 2))
    east_out[...] = sea * (east_out[...] + dot(lanes_to_rows, east_pick, precision=HIGHEST))
    north_out[...] = sea * (north_out[...] + dot(lanes_to_rows, north_pick, precision=HIGHEST))

    @pl.loop(1, n)
    def _(d):
        forcing_copy(lax.rem(me + d, n), d, me).wait_send()


def local(
    n,
    east_current,
    north_current,
    land_mask,
    spectrum,
    spectral_in,
    spectral_out,
    conv_first,
    conv_second,
    conv_last,
):
    rows, width = east_current.shape
    bins, columns, cells = spectrum.shape
    hid = spectral_in.shape[0]
    hc = conv_first.shape[0]
    assert columns == 2 and LANES % rows == 0 and rows >= 8
    assert width & (width - 1) == 0 and width % 32 == 0 and cells % LANES == 0
    wide = -(-width // LANES) * LANES
    speeds, drift, stress = bin_tables()
    vmem = pl.BlockSpec(memory_space=pltpu.VMEM)
    east, north, final = pl.pallas_call(
        functools.partial(kernel, n),
        out_shape=(
            jax.ShapeDtypeStruct((rows, width), F32),
            jax.ShapeDtypeStruct((rows, width), F32),
            jax.ShapeDtypeStruct((bins, columns, cells), BF16),
        ),
        in_specs=[vmem] * 12,
        out_specs=(vmem, vmem, vmem),
        scratch_shapes=[
            pltpu.VMEM((columns, bins, cells), BF16),
            pltpu.VMEM((2, bins, cells), BF16),
            pltpu.VMEM((2, bins, cells), BF16),
            pltpu.VMEM((columns, CHUNK, cells), F32),
            pltpu.VMEM((2, columns, hid, cells), BF16),
            pltpu.VMEM((columns, hid, cells), F32),
            pltpu.VMEM((8, cells), F32),
            pltpu.VMEM((n, 8, LANES), F32),
            pltpu.VMEM((n, 8, LANES), F32),
            pltpu.VMEM((cells // LANES, 8, LANES), F32),
            pltpu.VMEM((n, 8, LANES), F32),
            pltpu.VMEM((2, rows, wide), F32),
            pltpu.VMEM((2, 8, wide), F32),
            pltpu.VMEM((2, 8, wide), F32),
            pltpu.VMEM((24, (rows + 8) * width), F32),
            pltpu.VMEM((9 * hc, rows * width), BF16),
            pltpu.VMEM((columns, 16, cells), F32),
            pltpu.VMEM((columns, CHUNK, cells), BF16),
            pltpu.SemaphoreType.DMA((2, 2, CHUNKS)),
            pltpu.SemaphoreType.DMA((2, 2, CHUNKS)),
            pltpu.SemaphoreType.DMA((n,)),
            pltpu.SemaphoreType.DMA((n,)),
            pltpu.SemaphoreType.DMA((n,)),
            pltpu.SemaphoreType.DMA((n,)),
            pltpu.SemaphoreType.DMA((2,)),
            pltpu.SemaphoreType.DMA((2,)),
        ],
        compiler_params=pltpu.CompilerParams(
            collective_id=0, has_side_effects=True, vmem_limit_bytes=56 << 20
        ),
    )(
        east_current,
        north_current,
        land_mask,
        spectrum.transpose(1, 0, 2),
        spectral_in.T,
        spectral_out,
        conv_first.T,
        conv_second,
        conv_last,
        jnp.asarray(speeds),
        jnp.asarray(drift),
        jnp.asarray(stress),
    )
    return east, north, final


def solution(mesh):
    n = mesh.shape["gx"]
    in_specs = (
        P(("groups", "gx"), None),
        P(("groups", "gx"), None),
        P(("groups", "gx"), None),
        P(None, ("groups", "gx"), None),
        P(),
        P(),
        P(),
        P(),
        P(),
    )
    out_specs = (
        P(("groups", "gx"), None),
        P(("groups", "gx"), None),
        P(None, ("groups", "gx"), None),
    )
    return jax.shard_map(
        functools.partial(local, n), mesh=mesh, in_specs=in_specs, out_specs=out_specs, check_vma=False
    )
```

time: 124 us -> 58.5 us (0.47)
  Pallas kernels: 0 us -> 49.6 us
  starting transfers between devices: 43.9 us -> 0 us
  other arithmetic: 30.7 us -> 0 us
  local copies, waits for them, and re-layouts: 31.3 us -> 8 us
  matrix products: 13.9 us -> 0 us
  waiting for transfers between devices: 2.27 us -> 0 us
    pallas_call x0 -> x1, Pallas kernels: none -> 49.6 us  [local(): pl.pallas_call(functools.partial(kernel, n), out_shape=(jax.ShapeDtypeStr...]
    ppermute x8 -> x0, starting transfers between devices: 25 us -> none  [the longest x4 19.7 us: with_halo(): lax.ppermute(tail, axis, [(i, (i + 1) % count) for i in range(ends)])]
    all_to_all x2 -> x0, starting transfers between devices: 18.9 us -> none  [the longest x1 11.5 us: local(): lax.all_to_all(forcing, 'gx', split_axis=2, concat_axis=1, tiled=True)]
    dot_general x6 -> x0, matrix products: 13.9 us -> none  [the longest x2 8.42 us: wave_step(): jnp.dot(spectral_out, hidden, preferred_element_type=jnp.float32)]
    add x8 -> x0, other arithmetic: 13.5 us -> none  [the longest x4 12.2 us: divergence(): jnp.maximum(lower_speed, 0.0) * lower_energy]
    convert_element_type x5 -> x0, other arithmetic: 10.6 us -> none  [the longest x2 9.04 us: wave_step(): return (updated.astype(jnp.bfloat16), source)]
    convert_element_type x2 -> x0, local copies, waits for them, and re-layouts: 8.12 us -> none  [the longest x1 7.99 us: wave_step(): return (updated.astype(jnp.bfloat16), source)]
    unnamed x70 -> x4, local copies, waits for them, and re-layouts: 13 us -> 8 us
  transfers between devices with their start and end apart: 10 -> 0, of which waited for: 1 -> 0; matrix products, arithmetic and copies ran while one was open for 28% -> 0% of each run, Pallas kernels for 0% -> 0%
where the time goes in v1:
time: 58.5 us; the launch traced here: 58.2 us
  Pallas kernels  49.6 us (85%)
  local copies, waits for them, and re-layouts  8 us (14%)
  between operations  0.64 us (1%)
    pallas_call x1, Pallas kernels, local(): pl.pallas_call(functools.partial(kernel, n), out_shape=(jax.ShapeDtypeStr...  49.6 us
    unnamed x4, local copies, waits for them, and re-layouts  8 us

profile of v1, /device:TPU:0, one launch (start us, length us, event | category | flops | bytes accessed | tf_op | source)
XLA Modules:
  0.0 58.2 jit_solution(7570905734525515469)
XLA Ops:
  0.6 2.6 %copy.17 = bf16[1296,2,256]{2,0,1:T(8,128)(2,1)} copy(bf16[1296,2,256]{2,1,0:T(2,128)(2,1)} %param.15) | data formatting | bytes 2654208 | tf_op args[3]
  3.2 49.6 %shard_map.139 = (f32[16,32]{1,0:T(8,128)}, f32[16,32]{1,0:T(8,128)}, bf16[1296,2,256]{2,1,0:T(2,128)(2,1)}) custom-call(f32[16,32]{1,0:T(8,128)} %east_ref.1, f32[16,32]{1,0:T(8,128)} %north_ref.1, s32[16,32]{1,0:T(8,128)} %land_ref.1, bf16[2,1296,256]{2,1,0:T(8,128)(2,1)} %bitcast.5, bf16[1296,256]{1,0:T(8,128)(2,1)} %bitcast.6, ...), custom_call_target="tpu_custom_call" | custom-call | tf_op jit(solution)/shard_map/pallas_call | solution.py:497
  52.8 1.3 %copy.21 = f32[16,32]{1,0:T(8,128)} copy(f32[16,32]{1,0:T(8,128)} %get-tuple-element.6) | data formatting | bytes 4096
  54.1 1.3 %copy.22 = f32[16,32]{1,0:T(8,128)} copy(f32[16,32]{1,0:T(8,128)} %get-tuple-element.7) | data formatting | bytes 4096
  55.4 2.9 %copy.23 = bf16[1296,2,256]{2,1,0:T(2,128)(2,1)} copy(bf16[1296,2,256]{2,1,0:T(2,128)(2,1)} %get-tuple-element.8) | data formatting | bytes 2654208

commit v2 on v1

--- a/solution.py
+++ b/solution.py
@@ -87,8 +87,7 @@
     speeds_ref,
     drift_ref,
     stress_ref,
-    east_out,
-    north_out,
+    both_out,
     final_ref,
     first_ref,
     left_ref,
@@ -118,6 +117,7 @@
     ocean_recv_sem,
 ):
     me = lax.axis_index("gx")
+    east_out, north_out = both_out.at[0], both_out.at[1]
     has_left = me > 0
     has_right = me < n - 1
     rows, width = east_ref.shape
@@ -128,7 +128,7 @@
 
     barrier = pltpu.get_barrier_semaphore()
 
-    @pl.loop(1, n)
+    @pl.loop(1, n, unroll=True)
     def _(d):
         peer = lax.rem(me + d, n)
         pl.semaphore_signal(barrier, inc=1, device_id={"gx": peer}, device_id_type=MESH)
@@ -222,11 +222,11 @@
         def _():
             halo_copy(step, source, k, False).start()
 
+    @pl.loop(1, n, unroll=True)
+    def _(d):
+        current_copy(lax.rem(me + d, n), d, me).start()
+
     send_halo(0, energy_ref, 0)
-
-    @pl.loop(1, n)
-    def _(d):
-        current_copy(lax.rem(me + d, n), d, me).start()
 
     @pl.when(has_right)
     def _():
@@ -245,82 +245,7 @@
         hidden_ref[0, c] = jax.nn.gelu(z).astype(BF16)
     acc_ref[...] = jnp.zeros_like(acc_ref)
 
-    @pl.when(has_left)
-    def _():
-        ocean_copy(True).wait_recv()
-
-    @pl.when(has_right)
-    def _():
-        ocean_copy(False).wait_recv()
-
-    strip = rows + 8
-    flat = strip * width
-    lane = iota((wide, flat), 1)
-    spread = ones_where((lane & (width - 1)) == iota((wide, flat), 0), BF16)
-    ext_rows = rows + 16
-    start = (iota((ext_rows, flat), 0) - 4) * width
-    ahead = iota((ext_rows, flat), 1) - start
-    chosen = (ahead >= 0) & (ahead < width)
-    bends = []
-    lines = []
-    ext_r = iota((rows, ext_rows), 1)
-    ext_c = iota((rows, ext_rows), 0)
-    vertical = ones_where((ext_r == ext_c + 7) | (ext_r == ext_c + 9))
-    side_r = iota((wide, wide), 0)
-    side_c = iota((wide, wide), 1)
-    horizontal = ones_where(
-        ((side_r == side_c + 1) | (side_r == side_c - 1)) & (side_r < width) & (side_c < width)
-    )
-    for f in range(2):
-        own = own_ref[f]
-        ext = jnp.concatenate([up_ref[f], own, down_ref[f]], axis=0)
-        line = dot((INPUT_SCALE * ext).astype(BF16), spread)
-        lines.append(jnp.sum(jnp.where(chosen, line, 0.0), axis=0, keepdims=True))
-        bends.append(
-            dot(vertical, ext, precision=HIGHEST)
-            + dot(own, horizontal, precision=HIGHEST)
-            - 4.0 * own
-        )
-    sub = iota((8, flat), 0)
-    line8 = jnp.where(sub == 0, lines[0], jnp.where(sub == 1, lines[1], 0.0))
-
-    def shifted(x, dy, dx):
-        shape = x.shape
-        moved = dy * width + dx
-        y = pltpu.roll(x, (-moved) % flat, 1) if moved else x
-        if dx:
-            at = (iota(shape, 1) & (width - 1)) + dx
-            y = jnp.where((at >= 0) & (at < width), y, 0.0)
-        return y
-
-    taps = [(dy, dx) for dy in (-1, 0, 1) for dx in (-1, 0, 1)]
-    for t, (dy, dx) in enumerate(taps):
-        taps1[2 * t : 2 * t + 2] = shifted(line8, dy, dx)[0:2]
-    h1 = dot(conv1_ref[...], taps1[0:18].astype(BF16), ((0,), (0,)))
-    h1 = jnp.maximum(h1, 0.0).astype(BF16).astype(F32)
-    at = iota(h1.shape, 1) + (me * rows - 4) * width
-    h1 = jnp.where((at >= 0) & (at < n * rows * width), h1, 0.0)
-    hc = h1.shape[0]
-    for t, (dy, dx) in enumerate(taps):
-        moved = shifted(h1, dy, dx)[:, 4 * width : (4 + rows) * width]
-        taps2[hc * t : hc * t + hc] = moved.astype(BF16)
-    h2 = jnp.maximum(dot(conv2_ref[...], taps2[...]), 0.0).astype(BF16)
-    closure = dot(conv3_ref[...], h2)
-    body = rows * width
-    back = iota((body, wide), 0)
-    gather = ones_where((back & (width - 1)) == iota((body, wide), 1))
-    begun = iota((rows, body), 1) - iota((rows, body), 0) * width
-    mine = (begun >= 0) & (begun < width)
-    closures = [
-        dot(jnp.where(mine, closure[f : f + 1], 0.0), gather, precision=HIGHEST) for f in range(2)
-    ]
-    mu_w, mv_w = own_ref[0], own_ref[1]
-    east_part = mu_w + VISCOSITY * bends[0] + CORIOLIS * mv_w + closures[0]
-    north_part = mv_w + VISCOSITY * bends[1] - CORIOLIS * mu_w + closures[1]
-    east_out[...] = east_part[:, :width]
-    north_out[...] = north_part[:, :width]
-
-    @pl.loop(1, n)
+    @pl.loop(1, n, unroll=True)
     def _(d):
         sender = lax.rem(me + d, n)
         current_copy(me, d, sender).wait_recv()
@@ -403,6 +328,81 @@
         hidden_ref[1, c] = hidden
         stresses.append(dot(stress8, hidden.astype(F32), precision=HIGHEST))
 
+    @pl.when(has_left)
+    def _():
+        ocean_copy(True).wait_recv()
+
+    @pl.when(has_right)
+    def _():
+        ocean_copy(False).wait_recv()
+
+    strip = rows + 8
+    flat = strip * width
+    lane = iota((wide, flat), 1)
+    spread = ones_where((lane & (width - 1)) == iota((wide, flat), 0), BF16)
+    ext_rows = rows + 16
+    start = (iota((ext_rows, flat), 0) - 4) * width
+    ahead = iota((ext_rows, flat), 1) - start
+    chosen = (ahead >= 0) & (ahead < width)
+    bends = []
+    lines = []
+    ext_r = iota((rows, ext_rows), 1)
+    ext_c = iota((rows, ext_rows), 0)
+    vertical = ones_where((ext_r == ext_c + 7) | (ext_r == ext_c + 9))
+    side_r = iota((wide, wide), 0)
+    side_c = iota((wide, wide), 1)
+    horizontal = ones_where(
+        ((side_r == side_c + 1) | (side_r == side_c - 1)) & (side_r < width) & (side_c < width)
+    )
+    for f in range(2):
+        own = own_ref[f]
+        ext = jnp.concatenate([up_ref[f], own, down_ref[f]], axis=0)
+        line = dot((INPUT_SCALE * ext).astype(BF16), spread)
+        lines.append(jnp.sum(jnp.where(chosen, line, 0.0), axis=0, keepdims=True))
+        bends.append(
+            dot(vertical, ext, precision=HIGHEST)
+            + dot(own, horizontal, precision=HIGHEST)
+            - 4.0 * own
+        )
+    sub = iota((8, flat), 0)
+    line8 = jnp.where(sub == 0, lines[0], jnp.where(sub == 1, lines[1], 0.0))
+
+    def shifted(x, dy, dx):
+        shape = x.shape
+        moved = dy * width + dx
+        y = pltpu.roll(x, (-moved) % flat, 1) if moved else x
+        if dx:
+            at = (iota(shape, 1) & (width - 1)) + dx
+            y = jnp.where((at >= 0) & (at < width), y, 0.0)
+        return y
+
+    taps = [(dy, dx) for dy in (-1, 0, 1) for dx in (-1, 0, 1)]
+    for t, (dy, dx) in enumerate(taps):
+        taps1[2 * t : 2 * t + 2] = shifted(line8, dy, dx)[0:2]
+    h1 = dot(conv1_ref[...], taps1[0:18].astype(BF16), ((0,), (0,)))
+    h1 = jnp.maximum(h1, 0.0).astype(BF16).astype(F32)
+    at = iota(h1.shape, 1) + (me * rows - 4) * width
+    h1 = jnp.where((at >= 0) & (at < n * rows * width), h1, 0.0)
+    hc = h1.shape[0]
+    for t, (dy, dx) in enumerate(taps):
+        moved = shifted(h1, dy, dx)[:, 4 * width : (4 + rows) * width]
+        taps2[hc * t : hc * t + hc] = moved.astype(BF16)
+    h2 = jnp.maximum(dot(conv2_ref[...], taps2[...]), 0.0).astype(BF16)
+    closure = dot(conv3_ref[...], h2)
+    body = rows * width
+    back = iota((body, wide), 0)
+    gather = ones_where((back & (width - 1)) == iota((body, wide), 1))
+    begun = iota((rows, body), 1) - iota((rows, body), 0) * width
+    mine = (begun >= 0) & (begun < width)
+    closures = [
+        dot(jnp.where(mine, closure[f : f + 1], 0.0), gather, precision=HIGHEST) for f in range(2)
+    ]
+    mu_w, mv_w = own_ref[0], own_ref[1]
+    east_part = mu_w + VISCOSITY * bends[0] + CORIOLIS * mv_w + closures[0]
+    north_part = mv_w + VISCOSITY * bends[1] - CORIOLIS * mu_w + closures[1]
+    east_out[...] = east_part[:, :width]
+    north_out[...] = north_part[:, :width]
+
     @pl.loop(0, CHUNKS)
     def _(k):
         wave_chunk(1, first_ref, final_ref, k)
@@ -422,13 +422,13 @@
     for t in range(tiles):
         send_for[t] = packed[:, t * LANES : (t + 1) * LANES]
 
-    @pl.loop(1, n)
+    @pl.loop(1, n, unroll=True)
     def _(d):
         forcing_copy(lax.rem(me + d, n), d, me).start()
 
     recv_for[pl.ds(me, 1)] = send_for[pl.ds(lax.div(me * rows, LANES), 1)]
 
-    @pl.loop(1, n)
+    @pl.loop(1, n, unroll=True)
     def _(d):
         current_copy(lax.rem(me + d, n), d, me).wait_send()
 
@@ -452,7 +452,7 @@
             def _(step=step, source=source):
                 halo_copy(step, source, k, False).wait_send()
 
-    @pl.loop(1, n)
+    @pl.loop(1, n, unroll=True)
     def _(d):
         sender = lax.rem(me + d, n)
         forcing_copy(me, d, sender).wait_recv()
@@ -468,7 +468,7 @@
     east_out[...] = sea * (east_out[...] + dot(lanes_to_rows, east_pick, precision=HIGHEST))
     north_out[...] = sea * (north_out[...] + dot(lanes_to_rows, north_pick, precision=HIGHEST))
 
-    @pl.loop(1, n)
+    @pl.loop(1, n, unroll=True)
     def _(d):
         forcing_copy(lax.rem(me + d, n), d, me).wait_send()
 
@@ -494,15 +494,14 @@
     wide = -(-width // LANES) * LANES
     speeds, drift, stress = bin_tables()
     vmem = pl.BlockSpec(memory_space=pltpu.VMEM)
-    east, north, final = pl.pallas_call(
+    both, final = pl.pallas_call(
         functools.partial(kernel, n),
         out_shape=(
-            jax.ShapeDtypeStruct((rows, width), F32),
-            jax.ShapeDtypeStruct((rows, width), F32),
+            jax.ShapeDtypeStruct((2, rows, width), F32),
             jax.ShapeDtypeStruct((bins, columns, cells), BF16),
         ),
         in_specs=[vmem] * 12,
-        out_specs=(vmem, vmem, vmem),
+        out_specs=(vmem, vmem),
         scratch_shapes=[
             pltpu.VMEM((columns, bins, cells), BF16),
             pltpu.VMEM((2, bins, cells), BF16),
@@ -532,7 +531,7 @@
             pltpu.SemaphoreType.DMA((2,)),
         ],
         compiler_params=pltpu.CompilerParams(
-            collective_id=0, has_side_effects=True, vmem_limit_bytes=56 << 20
+            collective_id=0, has_side_effects=True, vmem_limit_bytes=20 * bins * cells + (16 << 20)
         ),
     )(
         east_current,
@@ -548,7 +547,7 @@
         jnp.asarray(drift),
         jnp.asarray(stress),
     )
-    return east, north, final
+    return both[0], both[1], final
 
 
 def solution(mesh):

time: 58.5 us -> 50.2 us (0.86)
  local copies, waits for them, and re-layouts: 8 us -> 3.48 us
  Pallas kernels: 49.6 us -> 45.8 us
    unnamed x4 -> x24, local copies, waits for them, and re-layouts: 8 us -> 2.88 us
    pallas_call x1, Pallas kernels: 49.6 us -> 45.8 us  [local(): pl.pallas_call(functools.partial(kernel, n), out_shape=(jax.ShapeDtypeStr...]
    squeeze x0 -> x1, local copies, waits for them, and re-layouts: none -> 0.61 us  [local(): return (both[0], both[1], final)]
where the time goes in v2:
time: 50.2 us; the launch traced here: 50.1 us
  Pallas kernels  45.8 us (91%)
  local copies, waits for them, and re-layouts  3.48 us (7%)
  between operations  0.77 us (2%)
    pallas_call x1, Pallas kernels, local(): pl.pallas_call(functools.partial(kernel, n), out_shape=(jax.ShapeDtypeStr...  45.8 us
    unnamed x24, local copies, waits for them, and re-layouts  2.88 us

profile of v2, /device:TPU:0, one launch (start us, length us, event | category | flops | bytes accessed | tf_op | source)
XLA Modules:
  0.0 50.1 jit_solution(16625071980137463486)
XLA Ops:
  0.6 0.0 copy-start
  0.6 0.0 copy-start.1
  0.7 0.0 copy-start.2
  0.7 0.0 copy-start.3
  0.7 0.0 copy-start.4
  0.7 0.0 copy-start.5
  0.7 0.0 copy-start.6
  0.7 0.0 copy-start.7
  0.7 0.0 copy-start.8
  0.7 0.0 copy-start.9
  0.7 0.0 copy-start.10
  0.8 1.6 %copy.17 = bf16[1296,2,256]{2,0,1:T(8,128)(2,1)S(1)} copy(bf16[1296,2,256]{2,1,0:T(2,128)(2,1)} %param.15) | data formatting | bytes 2654208 | tf_op args[3]
  2.4 0.0 copy-done
  2.4 0.0 copy-done.1
  2.4 0.1 copy-done.2
  2.5 0.0 copy-done.3
  2.5 0.0 copy-done.4
  2.5 0.0 copy-done.5
  2.5 0.0 copy-done.6
  2.5 0.0 copy-done.7
  2.6 0.0 copy-done.8
  2.6 0.0 copy-done.9
  2.6 0.0 copy-done.10
  2.6 45.8 %shard_map.139 = (f32[2,16,32]{2,1,0:T(8,128)S(1)}, bf16[1296,2,256]{2,1,0:T(2,128)(2,1)S(1)}) custom-call(f32[16,32]{1,0:T(8,128)S(1)} %copy-done.6, f32[16,32]{1,0:T(8,128)S(1)} %copy-done.7, s32[16,32]{1,0:T(8,128)S(1)} %copy-done.8, bf16[2,1296,256]{2,1,0:T(8,128)(2,1)S(1)} %bitcast.9, bf16[1296,256]{1,0:T(8,128)(2,1)S(1)} %bitcast.10, ...), custom_call_target="tpu_custom_call" | custom-call | tf_op jit(solution)/shard_map/pallas_call | solution.py:497
  48.4 0.6 %slice_bitcast_fusion = (f32[16,32]{1,0:T(8,128)}, f32[16,32]{1,0:T(8,128)}) fusion(f32[2,16,32]{2,1,0:T(8,128)S(1)} %get-tuple-element.5), kind=kLoop, calls=%fused_computation.1 | loop fusion | bytes 8192 | tf_op jit(solution)/shard_map/squeeze | solution.py:550
  49.0 1.1 %copy.19 = bf16[1296,2,256]{2,1,0:T(2,128)(2,1)} copy(bf16[1296,2,256]{2,1,0:T(2,128)(2,1)S(1)} %get-tuple-element.14) | data formatting | bytes 2654208
Async XLA Ops:
  0.6 1.8 %copy-start = (bf16[256,1296]{0,1:T(8,128)(2,1)S(1)}, bf16[256,1296]{0,1:T(8,128)(2,1)}, u32[]{:S(2)}) copy-start(bf16[256,1296]{0,1:T(8,128)(2,1)} %param.16) | copy-start | bytes 1990660
  0.6 1.8 %copy-start.1 = (bf16[1296,256]{1,0:T(8,128)(2,1)S(1)}, bf16[1296,256]{1,0:T(8,128)(2,1)}, u32[]{:S(2)}) copy-start(bf16[1296,256]{1,0:T(8,128)(2,1)} %wout_ref.1) | copy-start | bytes 1990660
  0.7 1.9 %copy-start.2 = (f32[1296,2]{1,0:T(8,128)S(1)}, f32[1296,2]{1,0:T(8,128)}, u32[]{:S(2)}) copy-start(f32[1296,2]{1,0:T(8,128)} %constant.6.clone.speeds_ref) | copy-start | bytes 31108
  0.7 1.9 %copy-start.3 = (bf16[64,576]{1,0:T(8,128)(2,1)S(1)}, bf16[64,576]{1,0:T(8,128)(2,1)}, u32[]{:S(2)}) copy-start(bf16[64,576]{1,0:T(8,128)(2,1)} %conv2_ref.1) | copy-start | bytes 221188
  0.7 1.9 %copy-start.4 = (bf16[9,16,144]{2,1,0:T(8,128)(2,1)S(1)}, bf16[9,16,144]{2,1,0:T(8,128)(2,1)}, u32[]{:S(2)}) copy-start(bf16[9,16,144]{2,1,0:T(8,128)(2,1)} %constant.7.clone.drift_ref) | copy-start | bytes 124420
  0.7 1.9 %copy-start.5 = (bf16[16,1296]{1,0:T(8,128)(2,1)S(1)}, bf16[16,1296]{1,0:T(8,128)(2,1)}, u32[]{:S(2)}) copy-start(bf16[16,1296]{1,0:T(8,128)(2,1)} %constant.8.clone.stress_ref) | copy-start | bytes 124420
  0.7 1.8 %copy-start.6 = (f32[16,32]{1,0:T(8,128)S(1)}, f32[16,32]{1,0:T(8,128)}, u32[]{:S(2)}) copy-start(f32[16,32]{1,0:T(8,128)} %east_ref.1) | copy-start | bytes 6148
  0.7 1.8 %copy-start.7 = (f32[16,32]{1,0:T(8,128)S(1)}, f32[16,32]{1,0:T(8,128)}, u32[]{:S(2)}) copy-start(f32[16,32]{1,0:T(8,128)} %north_ref.1) | copy-start | bytes 6148
  0.7 1.8 %copy-start.8 = (s32[16,32]{1,0:T(8,128)S(1)}, s32[16,32]{1,0:T(8,128)}, u32[]{:S(2)}) copy-start(s32[16,32]{1,0:T(8,128)} %land_ref.1) | copy-start | bytes 6148
  0.7 1.8 %copy-start.9 = (bf16[64,18]{0,1:T(8,128)(2,1)S(1)}, bf16[64,18]{0,1:T(8,128)(2,1)}, u32[]{:S(2)}) copy-start(bf16[64,18]{0,1:T(8,128)(2,1)} %param.18) | copy-start | bytes 6916
  0.7 1.8 %copy-start.10 = (bf16[2,64]{1,0:T(2,128)(2,1)S(1)}, bf16[2,64]{1,0:T(2,128)(2,1)}, u32[]{:S(2)}) copy-start(bf16[2,64]{1,0:T(2,128)(2,1)} %conv3_ref.1) | copy-start | bytes 772
